TPU v7x, 32 devices: a whole 2x2x4 slice. The times are simulated.
32 devices in a mesh: grp: 4 (over y, x), cp: 8 (over z, core).
Axes of the slice: x: 2, y: 2, z: 4, core: 2. Of those that a mesh axis runs over, the one named last changes fastest.
Arguments:
- queries: bfloat16 [4, 4096, 4096], P(None, ('grp', 'cp')), may hold values from -6 to 6, as said below
- keys: bfloat16 [4, 4096, 1024], P(None, ('grp', 'cp')), may hold values from -6 to 6, as said below
- values: bfloat16 [4, 4096, 1024], P(None, ('grp', 'cp')), may hold values from -6 to 6
- doc_lengths: int32 [4, 16], replicated, may hold values from 1 to 1024, 4096 in all within a row
Outputs:
- attended: bfloat16 [4, 4096, 4096], P(None, ('grp', 'cp'))
Inputs may be any that keep to these rules, and one draw needn't show every extreme that they name: `doc_lengths`: each row holds the lengths of 16 documents that fill the stream's 4096 tokens exactly; the longest is exactly 1024 tokens. `queries`: entries of order one. `keys`: entries of order one.
All inputs are finite; a program needn't handle non-finite values.
Results may differ from a plain program's by a relative error of at most 0.0038.
Values may be sent and summed in bfloat16 or wider, within the bound.
A program may use at most 128 MiB of HBM per device.

v0:
```python
import jax
import jax.numpy as jnp
from jax import lax
from jax.sharding import PartitionSpec as P

QUERY_HEADS = 32
KEY_VALUE_HEADS = 8
HEAD_WIDTH = 128


NEGATIVE = -1e30


def doc_of(positions, ends):
    return jnp.sum((positions[:, None] >= ends[None, :]).astype(jnp.int32), axis=1)


def doc_first(positions, ends):
    return jnp.max(jnp.where(ends[None, :] <= positions[:, None], ends[None, :], 0), axis=1)


def absorb(state, scores, allowed, value_portion):
    running_max, running_sum, running_acc = state
    scores = jnp.where(allowed, scores, NEGATIVE)
    new_max = jnp.maximum(running_max, jnp.max(scores, axis=-1))
    factor = jnp.exp(running_max - new_max)
    probs = jnp.where(allowed, jnp.exp(scores - new_max[..., None]), 0.0)
    new_sum = running_sum * factor + jnp.sum(probs, axis=-1)
    product = jnp.einsum(
        "hqk,khd->hqd",
        probs.astype(jnp.bfloat16),
        value_portion,
        preferred_element_type=jnp.float32,
    )
    return (new_max, new_sum, running_acc * factor[..., None] + product)


def attend_stream(query_seq, key_seq, value_seq, ends):
    stream_len = query_seq.shape[0]
    items = query_seq.shape[1]
    scale = HEAD_WIDTH ** (-0.5)
    positions = jnp.arange(stream_len, dtype=jnp.int32)
    all_docs = doc_of(positions, ends)
    all_firsts = doc_first(positions, ends)
    span = min(512, stream_len)
    spans = stream_len // span

    def query_span(number):
        begin = number * span
        query_tile = lax.dynamic_slice_in_dim(query_seq, begin, span, 0)
        query_pos = lax.dynamic_slice_in_dim(positions, begin, span, 0)
        query_doc = lax.dynamic_slice_in_dim(all_docs, begin, span, 0)
        first_span = lax.dynamic_index_in_dim(all_firsts, begin, 0, keepdims=False) // span

        def key_span(other, state):
            offset = other * span
            key_tile = lax.dynamic_slice_in_dim(key_seq, offset, span, 0)
            value_tile = lax.dynamic_slice_in_dim(value_seq, offset, span, 0)
            key_pos = lax.dynamic_slice_in_dim(positions, offset, span, 0)
            key_doc = lax.dynamic_slice_in_dim(all_docs, offset, span, 0)
            allowed = (key_pos[None, :] <= query_pos[:, None]) & (
                key_doc[None, :] == query_doc[:, None]
            )
            scores = (
                jnp.einsum("qhd,khd->hqk", query_tile, key_tile, preferred_element_type=jnp.float32)
                * scale
            )
            return absorb(state, scores, allowed, value_tile)

        start_state = (
            jnp.full((items, span), NEGATIVE, jnp.float32),
            jnp.zeros((items, span), jnp.float32),
            jnp.zeros((items, span, HEAD_WIDTH), jnp.float32),
        )
        final_max, final_sum, final_acc = lax.fori_loop(
            first_span, number + 1, key_span, start_state
        )
        return (final_acc / final_sum[..., None]).transpose(1, 0, 2).astype(jnp.bfloat16)

    tiles = lax.map(query_span, jnp.arange(spans, dtype=jnp.int32))
    return tiles.reshape(stream_len, items, HEAD_WIDTH)


def on_device(queries, keys, values, doc_lengths):
    n_ranks = lax.axis_size("cp")
    n_streams = queries.shape[0]
    rows_per = queries.shape[1]
    group_count = QUERY_HEADS // KEY_VALUE_HEADS
    per_rank = QUERY_HEADS // n_ranks
    stream_id = lax.axis_index("grp")
    lengths_row = lax.dynamic_index_in_dim(doc_lengths, stream_id, 0, keepdims=False)
    ends = jnp.cumsum(lengths_row)

    def by_heads(array):
        shaped = array.reshape(n_streams, rows_per, n_ranks, per_rank, HEAD_WIDTH)
        return shaped.transpose(0, 2, 1, 3, 4).reshape(
            n_streams * n_ranks, rows_per, per_rank, HEAD_WIDTH
        )

    key_wide = jnp.repeat(
        keys.reshape(n_streams, rows_per, KEY_VALUE_HEADS, HEAD_WIDTH), group_count, axis=2
    )
    value_wide = jnp.repeat(
        values.reshape(n_streams, rows_per, KEY_VALUE_HEADS, HEAD_WIDTH), group_count, axis=2
    )
    query_split = by_heads(queries)
    key_divided_rows = by_heads(key_wide)
    value_divided_rows = by_heads(value_wide)
    query_part = lax.all_to_all(query_split, ("grp", "cp"), split_axis=0, concat_axis=1, tiled=True)
    key_portion = lax.all_to_all(
        key_divided_rows, ("grp", "cp"), split_axis=0, concat_axis=1, tiled=True
    )
    value_portion = lax.all_to_all(
        value_divided_rows, ("grp", "cp"), split_axis=0, concat_axis=1, tiled=True
    )
    outcome = attend_stream(query_part[0], key_portion[0], value_portion[0], ends)
    head_output = outcome[None]
    returned = lax.all_to_all(head_output, ("grp", "cp"), split_axis=1, concat_axis=0, tiled=True)
    shaped = returned.reshape(n_streams, n_ranks, rows_per, per_rank, HEAD_WIDTH).transpose(
        0, 2, 1, 3, 4
    )
    return shaped.reshape(n_streams, rows_per, QUERY_HEADS * HEAD_WIDTH)


def solution(mesh):
    placed = (
        P(None, ("grp", "cp"), None),
        P(None, ("grp", "cp"), None),
        P(None, ("grp", "cp"), None),
        P(),
    )
    return jax.shard_map(
        on_device,
        mesh=mesh,
        in_specs=placed,
        out_specs=P(None, ("grp", "cp"), None),
        check_vma=False,
    )
```

profile of v0, /device:TPU:0, one launch (start us, length us, event | category | flops | bytes accessed | tf_op | source)
XLA Modules:
  0.0 612.2 jit_solution(1649393750826481190)
XLA Ops:
  0.0 7.8 %reshape.77 = bf16[4,128,8,4,128]{4,3,2,1,0:T(4,128)(2,1)} reshape(bf16[4,128,4096]{2,1,0:T(8,128)(2,1)} %param.8) | data formatting | bytes 8388608 | tf_op jit(solution)/shard_map/reshape | solution.py:95
  7.8 5.7 copy.49
  13.5 7.4 %all-to-all-start = ((bf16[32,128,4,128]{3,1,2,0:T(8,128)(2,1)}), bf16[32,128,4,128]{3,1,2,0:T(8,128)(2,1)}, u32[]{:S(2)}, u32[]{:S(2)}) async-start(bf16[32,128,4,128]{3,1,2,0:T(8,128)(2,1)} %bitcast.71), calls=%async_computation | async-start | bytes 8388608 | tf_op jit(solution)/shard_map/all_to_all | solution.py:109
  21.3 94.8 %all-to-all-done = bf16[32,128,4,128]{3,1,2,0:T(8,128)(2,1)} async-done(((bf16[32,128,4,128]{3,1,2,0:T(8,128)(2,1)}), bf16[32,128,4,128]{3,1,2,0:T(8,128)(2,1)}, u32[]{:S(2)}, u32[]{:S(2)}) %all-to-all-start) | async-done | bytes 4194336 | tf_op jit(solution)/shard_map/all_to_all | solution.py:109
  116.0 3.1 broadcast_in_dim.53
  119.1 3.7 all-to-all-start.2
  123.1 94.8 %all-to-all-done.2 = bf16[32,128,4,128]{3,1,2,0:T(8,128)(2,1)} async-done(((bf16[32,128,4,128]{3,1,2,0:T(8,128)(2,1)}), bf16[32,128,4,128]{3,1,2,0:T(8,128)(2,1)}, u32[]{:S(2)}, u32[]{:S(2)}) %all-to-all-start.2) | async-done | bytes 4194336 | tf_op jit(solution)/shard_map/all_to_all | solution.py:113
  217.9 3.0 broadcast_in_dim.52
  220.9 3.6 all-to-all-start.1
  225.6 4.7 copy.50
  230.3 4.7 copy.54
  235.0 84.5 %all-to-all-done.1 = bf16[32,128,4,128]{3,1,2,0:T(8,128)(2,1)} async-done(((bf16[32,128,4,128]{3,1,2,0:T(8,128)(2,1)}), bf16[32,128,4,128]{3,1,2,0:T(8,128)(2,1)}, u32[]{:S(2)}, u32[]{:S(2)}) %all-to-all-start.1) | async-done | bytes 4194336 | tf_op jit(solution)/shard_map/all_to_all | solution.py:110
  319.5 4.7 copy.52
  324.3 170.2 %while.41 = (s32[]{:T(128)}, bf16[8,512,4,128]{3,1,0,2:T(8,128)(2,1)}, s32[8]{0:T(128)S(1)}, s32[4096]{0:T(1024)S(1)}, s32[4096]{0:T(1024)S(1)}, /*index=5*/s32[...) while((s32[]{:T(128)}, ...), condition=%wide.region_8.9_spmd.clone, body=%wide.region_3.8_spmd.clone.sunk | while | flops 552341504 | bytes 21153056 | solution.py:80
  330.8 6.4 %while.42 = (s32[]{:T(128)}, f32[4,512]{1,0:T(4,128)S(1)}, f32[4,512]{1,0:T(4,128)S(1)}, f32[4,512,128]{2,1,0:T(8,128)S(1)}, s32[]{:T(128)}, /*index=5*/s32[4096...) while((s32[]{:T(128)}, f32[4,512]{1,0:T(4,128)S(1)}, ...), condition=%wide.region_7.7_spmd, body=%wide.region_4.6_spmd.sunk | while | flops 551817216 | bytes 17449172 | solution.py:75
  334.3 2.9 fusion.31
  344.9 12.8 %while.42 = (s32[]{:T(128)}, f32[4,512]{1,0:T(4,128)S(1)}, f32[4,512]{1,0:T(4,128)S(1)}, f32[4,512,128]{2,1,0:T(8,128)S(1)}, s32[]{:T(128)}, /*index=5*/s32[4096...) while((s32[]{:T(128)}, f32[4,512]{1,0:T(4,128)S(1)}, ...), condition=%wide.region_7.7_spmd, body=%wide.region_4.6_spmd.sunk | while | flops 551817216 | bytes 17449172 | solution.py:75
  348.4 2.9 fusion.31
  354.8 2.9 fusion.31
  365.4 19.2 %while.42 = (s32[]{:T(128)}, f32[4,512]{1,0:T(4,128)S(1)}, f32[4,512]{1,0:T(4,128)S(1)}, f32[4,512,128]{2,1,0:T(8,128)S(1)}, s32[]{:T(128)}, /*index=5*/s32[4096...) while((s32[]{:T(128)}, f32[4,512]{1,0:T(4,128)S(1)}, ...), condition=%wide.region_7.7_spmd, body=%wide.region_4.6_spmd.sunk | while | flops 551817216 | bytes 17449172 | solution.py:75
  365.8 1.9 fusion.29
  368.9 2.9 fusion.31
  375.2 2.9 fusion.31
  381.6 2.9 fusion.31
  392.2 12.8 %while.42 = (s32[]{:T(128)}, f32[4,512]{1,0:T(4,128)S(1)}, f32[4,512]{1,0:T(4,128)S(1)}, f32[4,512,128]{2,1,0:T(8,128)S(1)}, s32[]{:T(128)}, /*index=5*/s32[4096...) while((s32[]{:T(128)}, f32[4,512]{1,0:T(4,128)S(1)}, ...), condition=%wide.region_7.7_spmd, body=%wide.region_4.6_spmd.sunk | while | flops 551817216 | bytes 17449172 | solution.py:75
  392.7 1.9 fusion.29
  395.7 2.9 fusion.31
  402.1 2.9 fusion.31
  412.7 19.2 %while.42 = (s32[]{:T(128)}, f32[4,512]{1,0:T(4,128)S(1)}, f32[4,512]{1,0:T(4,128)S(1)}, f32[4,512,128]{2,1,0:T(8,128)S(1)}, s32[]{:T(128)}, /*index=5*/s32[4096...) while((s32[]{:T(128)}, f32[4,512]{1,0:T(4,128)S(1)}, ...), condition=%wide.region_7.7_spmd, body=%wide.region_4.6_spmd.sunk | while | flops 551817216 | bytes 17449172 | solution.py:75
  413.2 1.9 fusion.29
  416.2 2.9 fusion.31
  422.6 2.9 fusion.31
  429.0 2.9 fusion.31
  439.5 12.8 %while.42 = (s32[]{:T(128)}, f32[4,512]{1,0:T(4,128)S(1)}, f32[4,512]{1,0:T(4,128)S(1)}, f32[4,512,128]{2,1,0:T(8,128)S(1)}, s32[]{:T(128)}, /*index=5*/s32[4096...) while((s32[]{:T(128)}, f32[4,512]{1,0:T(4,128)S(1)}, ...), condition=%wide.region_7.7_spmd, body=%wide.region_4.6_spmd.sunk | while | flops 551817216 | bytes 17449172 | solution.py:75
  440.0 1.9 fusion.29
  443.0 2.9 fusion.31
  449.4 2.9 fusion.31
  460.0 12.8 %while.42 = (s32[]{:T(128)}, f32[4,512]{1,0:T(4,128)S(1)}, f32[4,512]{1,0:T(4,128)S(1)}, f32[4,512,128]{2,1,0:T(8,128)S(1)}, s32[]{:T(128)}, /*index=5*/s32[4096...) while((s32[]{:T(128)}, f32[4,512]{1,0:T(4,128)S(1)}, ...), condition=%wide.region_7.7_spmd, body=%wide.region_4.6_spmd.sunk | while | flops 551817216 | bytes 17449172 | solution.py:75
  463.5 2.9 fusion.31
  469.9 2.9 fusion.31
  480.5 12.8 %while.42 = (s32[]{:T(128)}, f32[4,512]{1,0:T(4,128)S(1)}, f32[4,512]{1,0:T(4,128)S(1)}, f32[4,512,128]{2,1,0:T(8,128)S(1)}, s32[]{:T(128)}, /*index=5*/s32[4096...) while((s32[]{:T(128)}, f32[4,512]{1,0:T(4,128)S(1)}, ...), condition=%wide.region_7.7_spmd, body=%wide.region_4.6_spmd.sunk | while | flops 551817216 | bytes 17449172 | solution.py:75
  484.0 2.9 fusion.31
  490.4 2.9 fusion.31
  494.4 5.8 copy.56
  500.2 96.8 %all_to_all.16 = bf16[1,4096,4,128]{3,2,0,1:T(4,128)(2,1)S(1)} all-to-all(bf16[1,4096,4,128]{3,2,0,1:T(4,128)(2,1)S(1)} %copy.56), channel_id=1, replica_groups=mesh['grp'=4,'cp'=8] {'grp','cp'}, dimensions={1} | all-to-all | bytes 8388608 | tf_op jit(solution)/shard_map/all_to_all | solution.py:118
  597.0 2.6 copy.57
  599.5 6.2 %copy.58 = bf16[4,128,8,4,128]{1,4,3,2,0:T(8,128)(2,1)} copy(bf16[4,128,8,4,128]{4,1,2,0,3:T(8,128)(2,1)} %bitcast.72) | data formatting | bytes 8388608 | tf_op jit(solution)/shard_map/transpose | solution.py:119
  605.7 6.4 %copy.59 = bf16[4,128,4096]{2,1,0:T(8,128)(2,1)} copy(bf16[4,128,4096]{1,2,0:T(8,128)(2,1)} %bitcast.73) | data formatting | bytes 8388608 | tf_op jit(solution)/shard_map/reshape | solution.py:122
  (220 shorter events, 82.2 us)
Async XLA Ops:
  0.0 21.0 %copy-start = (bf16[4,128,1024]{2,1,0:T(8,128)(2,1)S(1)}, bf16[4,128,1024]{2,1,0:T(8,128)(2,1)}, u32[]{:S(2)}) copy-start(bf16[4,128,1024]{2,1,0:T(8,128)(2,1)} %param.10) | copy-start | bytes 3145732
  13.5 102.5 %all-to-all-start = ((bf16[32,128,4,128]{3,1,2,0:T(8,128)(2,1)}), bf16[32,128,4,128]{3,1,2,0:T(8,128)(2,1)}, u32[]{:S(2)}, u32[]{:S(2)}) async-start(bf16[32,128,4,128]{3,1,2,0:T(8,128)(2,1)} %bitcast.71), calls=%async_computation | async-start | bytes 8388608 | tf_op jit(solution)/shard_map/all_to_all | solution.py:109
  119.1 3.7 copy-start.2
  119.1 98.8 %all-to-all-start.2 = ((bf16[32,128,4,128]{3,1,2,0:T(8,128)(2,1)}), bf16[32,128,4,128]{3,1,2,0:T(8,128)(2,1)}, u32[]{:S(2)}, u32[]{:S(2)}) async-start(bf16[32,128,4,128]{3,1,2,0:T(8,128)(2,1)} %bitcast.70), calls=%async_computation.2 | async-start | bytes 8388608 | tf_op jit(solution)/shard_map/all_to_all | solution.py:113
  220.9 98.7 %all-to-all-start.1 = ((bf16[32,128,4,128]{3,1,2,0:T(8,128)(2,1)}), bf16[32,128,4,128]{3,1,2,0:T(8,128)(2,1)}, u32[]{:S(2)}, u32[]{:S(2)}) async-start(bf16[32,128,4,128]{3,1,2,0:T(8,128)(2,1)} %bitcast.69), calls=%async_computation.1 | async-start | bytes 8388608 | tf_op jit(solution)/shard_map/all_to_all | solution.py:110
  605.7 6.4 %copy-start.1 = (bf16[4,128,1024]{2,1,0:T(8,128)(2,1)S(1)}, bf16[4,128,1024]{2,1,0:T(8,128)(2,1)}, u32[]{:S(2)}) copy-start(bf16[4,128,1024]{2,1,0:T(8,128)(2,1)} %param.10) | copy-start | bytes 3145732
where the time goes:
time: 616 us; the launch traced here: 612 us
  waiting for transfers between devices  274 us (44%)
  blocking collectives  96.8 us (16%)
  matrix products  81.7 us (13%)
  local copies, waits for them, and re-layouts  79.3 us (13%)
  loops' own time  33 us (5%)
  other arithmetic  32.6 us (5%)
  starting transfers between devices  14.7 us (2%)
    all_to_all x1, blocking collectives, on_device(): lax.all_to_all(head_output, ('grp', 'cp'), split_axis=1, concat_axis=0, t...  96.8 us
    all_to_all x1, waiting for transfers between devices, on_device(): lax.all_to_all(value_divided_rows, ('grp', 'cp'), split_axis=0, concat_ax...  94.8 us
    all_to_all x1, waiting for transfers between devices, on_device(): lax.all_to_all(query_split, ('grp', 'cp'), split_axis=0, concat_axis=1, t...  94.8 us
    all_to_all x1, waiting for transfers between devices, on_device(): lax.all_to_all(key_divided_rows, ('grp', 'cp'), split_axis=0, concat_axis...  84.5 us
    dot_general x17, matrix products, absorb(): jnp.einsum('hqk,khd->hqd', probs.astype(jnp.bfloat16), value_portion, pre...  48.9 us
    dot_general x17, matrix products, key_span(): jnp.einsum('qhd,khd->hqk', query_tile, key_tile, preferred_element_type=j...  32.7 us
    another operation x1, loops' own time, attend_stream(): tiles = lax.map(query_span, jnp.arange(spans, dtype=jnp.int32))  31.8 us
    reduce_sum x17, other arithmetic, absorb(): new_sum = running_sum * factor + jnp.sum(probs, axis=-1)  18 us
  transfers between devices with their start and end apart: 3, of which 3 were waited for; matrix products, arithmetic and copies ran while one was open for 2% of the time, Pallas kernels for 0%

commit v1 on v0

--- a/solution.py
+++ b/solution.py
@@ -1,14 +1,262 @@
+import functools
+
 import jax
 import jax.numpy as jnp
 from jax import lax
+from jax.experimental import pallas as pl
+from jax.experimental.pallas import tpu as pltpu
 from jax.sharding import PartitionSpec as P
+
+MESH = pl.DeviceIdType.MESH
+PARTS = 2
+WINDOW_BYTES = 40 * 2**20
 
 QUERY_HEADS = 32
 KEY_VALUE_HEADS = 8
 HEAD_WIDTH = 128
-
-
 NEGATIVE = -1e30
+LOG2_E = 1.4426950408889634
+
+
+def window_kernel(
+    n_grp, n_cp, streams, q_ref, k_ref, v_ref, len_ref, o_ref, kv, bias, local_sem, send_sem, recv_sem
+):
+    grp, cp = lax.axis_index("grp"), lax.axis_index("cp")
+    z, core = cp // 2, cp % 2
+    nz = n_cp // 2
+    chunks = streams * PARTS
+    rows = k_ref.shape[1]
+    part = k_ref.shape[2] // PARTS
+    heads = part // HEAD_WIDTH
+    group = QUERY_HEADS // KEY_VALUE_HEADS
+    partner = (grp, z * 2 + 1 - core)
+    up = (grp, cp + 2)
+    down = (grp, cp - 2)
+    next_line = ((grp + 1) % n_grp, cp)
+    prev_line = ((grp + n_grp - 1) % n_grp, cp)
+    fwd_row, hop_row, bwd_row, mate_row = 0, nz - 1, nz - 2, 2 * nz - 1
+
+    def local(ch, which):
+        source = (k_ref, v_ref)[which]
+        cols = pl.ds(pl.multiple_of((ch % PARTS) * part, part), part)
+        return pltpu.make_async_copy(
+            source.at[ch // PARTS, :, cols],
+            kv.at[0, ch, :, pl.ds(which * part, part)],
+            local_sem.at[which, ch],
+        )
+
+    def remote(source, target, ch, row, device):
+        return pltpu.make_async_remote_copy(
+            src_ref=kv.at[source, ch],
+            dst_ref=kv.at[target, ch],
+            send_sem=send_sem.at[row, ch],
+            recv_sem=recv_sem.at[target, ch],
+            device_id=device,
+            device_id_type=MESH,
+        )
+
+    def arrived(slot, ch):
+        remote(slot, slot, ch, 0, partner).wait_recv()
+
+    @pl.loop(0, chunks)
+    def _(ch):
+        local(ch, 0).start()
+        local(ch, 1).start()
+
+    barrier = pltpu.get_barrier_semaphore()
+
+    def greet(device):
+        pl.semaphore_signal(barrier, inc=1, device_id=device, device_id_type=MESH)
+
+    greet(partner)
+    greet(next_line)
+    greet(prev_line)
+
+    @pl.when(z < nz - 1)
+    def _():
+        greet(up)
+
+    @pl.when(z > 0)
+    def _():
+        greet(down)
+
+    at_end = (z == 0) | (z == nz - 1)
+    pl.semaphore_wait(barrier, jnp.where(at_end, 4, 5))
+
+    def to_partner(d, ch):
+        if d < nz:
+
+            @pl.when(core == 0)
+            def _():
+                remote(2 * d, 2 * d + 1, ch, mate_row + d, partner).start()
+
+        if d > 0:
+
+            @pl.when(core == 1)
+            def _():
+                remote(2 * d, 2 * d - 1, ch, mate_row + d, partner).start()
+
+    def attend(ch):
+        stream, piece = ch // PARTS, ch % PARTS
+        base = (grp * n_cp + cp) * rows
+        row = lax.broadcasted_iota(jnp.int32, (rows, rows), 0)
+        lane = lax.broadcasted_iota(jnp.int32, (rows, rows), 1)
+        first = jnp.zeros((rows, rows), jnp.int32)
+        end = jnp.int32(0)
+        for doc in range(len_ref.shape[1]):
+            end = end + len_ref[stream, doc]
+            first = jnp.maximum(first, jnp.where(row + base >= end, end, 0))
+        for r in range(n_cp + 1):
+            allowed = lane + (base - r * rows) >= first
+            if r == 0:
+                allowed = allowed & (lane <= row)
+            bias[:, r * rows : (r + 1) * rows] = jnp.where(allowed, 0.0, NEGATIVE)
+
+        @pl.loop(0, heads)
+        def _(head):
+            k_cols = pl.ds(pl.multiple_of(head * HEAD_WIDTH, HEAD_WIDTH), HEAD_WIDTH)
+            v_cols = pl.ds(pl.multiple_of(part + head * HEAD_WIDTH, HEAD_WIDTH), HEAD_WIDTH)
+            k_all = jnp.concatenate([kv[r, ch, :, k_cols] for r in range(n_cp + 1)], axis=0)
+            v_all = jnp.concatenate([kv[r, ch, :, v_cols] for r in range(n_cp + 1)], axis=0)
+            for j in range(group):
+                at = ((piece * heads + head) * group + j) * HEAD_WIDTH
+                q_cols = pl.ds(pl.multiple_of(at, HEAD_WIDTH), HEAD_WIDTH)
+                scores = lax.dot_general(
+                    q_ref[stream, :, q_cols],
+                    k_all,
+                    (((1,), (1,)), ((), ())),
+                    preferred_element_type=jnp.float32,
+                )
+                scores = scores + bias[...]
+                largest = jnp.max(scores, axis=1, keepdims=True)
+                probs = jnp.exp2((scores - largest) * (HEAD_WIDTH**-0.5 * LOG2_E))
+                total = jnp.sum(probs, axis=1, keepdims=True)
+                summed = jnp.dot(
+                    probs.astype(jnp.bfloat16), v_all, preferred_element_type=jnp.float32
+                )
+                o_ref[stream, :, q_cols] = (summed / total).astype(o_ref.dtype)
+
+    @pl.loop(0, chunks + nz)
+    def _(t):
+        @pl.when(t < chunks)
+        def _():
+            local(t, 0).wait()
+            local(t, 1).wait()
+            remote(0, 2 * nz, t, hop_row, next_line).start()
+
+            @pl.when(z < nz - 1)
+            def _():
+                remote(0, 2, t, fwd_row, up).start()
+
+            to_partner(0, t)
+
+        for d in range(nz, 0, -1):
+            ch = t - (nz + 1 - d)
+
+            @pl.when((ch >= 0) & (ch < chunks) & (z < d))
+            def _():
+                arrived(2 * d, ch)
+                if d > 1:
+
+                    @pl.when(z > 0)
+                    def _():
+                        remote(2 * d, 2 * d - 2, ch, bwd_row + d, down).start()
+
+                to_partner(d, ch)
+
+        for d in range(1, nz):
+            ch = t - d
+
+            @pl.when((ch >= 0) & (ch < chunks) & (z >= d))
+            def _():
+                arrived(2 * d, ch)
+                if d < nz - 1:
+
+                    @pl.when(z < nz - 1)
+                    def _():
+                        remote(2 * d, 2 * d + 2, ch, fwd_row + d, up).start()
+
+                to_partner(d, ch)
+
+        @pl.when(t >= nz)
+        def _():
+            ch = t - nz
+            for d in range(nz):
+                arrived(2 * d + 1, ch)
+            attend(ch)
+
+    @pl.loop(0, chunks)
+    def _(ch):
+        def sent(row):
+            remote(0, 1, ch, row, partner).wait_send()
+
+        sent(hop_row)
+        for d in range(nz - 1):
+
+            @pl.when((z >= d) & (z < nz - 1))
+            def _():
+                sent(fwd_row + d)
+
+        for d in range(2, nz + 1):
+
+            @pl.when((z < d) & (z > 0))
+            def _():
+                sent(bwd_row + d)
+
+        for d in range(nz + 1):
+            if d == 0:
+
+                @pl.when(core == 0)
+                def _():
+                    sent(mate_row)
+
+            elif d == nz:
+
+                @pl.when(core == 1)
+                def _():
+                    sent(mate_row + nz)
+
+            else:
+                sent(mate_row + d)
+
+
+def by_window(n_grp, n_cp, queries, keys, values, doc_lengths):
+    streams, rows, _ = queries.shape
+    chunks = streams * PARTS
+    width = 2 * keys.shape[2] // PARTS
+    window = (n_cp + 1) * rows
+    nz = n_cp // 2
+    pairs = streams * QUERY_HEADS * rows * window
+    return pl.pallas_call(
+        functools.partial(window_kernel, n_grp, n_cp, streams),
+        out_shape=jax.ShapeDtypeStruct(queries.shape, queries.dtype),
+        in_specs=[
+            pl.BlockSpec(memory_space=pltpu.VMEM),
+            pl.BlockSpec(memory_space=pl.ANY),
+            pl.BlockSpec(memory_space=pl.ANY),
+            pl.BlockSpec(memory_space=pltpu.SMEM),
+        ],
+        out_specs=pl.BlockSpec(memory_space=pltpu.VMEM),
+        scratch_shapes=[
+            pltpu.VMEM((n_cp + 1, chunks, rows, width), keys.dtype),
+            pltpu.VMEM((rows, window), jnp.float32),
+            pltpu.SemaphoreType.DMA((2, chunks)),
+            pltpu.SemaphoreType.DMA((3 * nz, chunks)),
+            pltpu.SemaphoreType.DMA((n_cp + 1, chunks)),
+        ],
+        cost_estimate=pl.CostEstimate(
+            flops=4 * pairs * HEAD_WIDTH, bytes_accessed=5 * queries.size, transcendentals=pairs
+        ),
+        compiler_params=pltpu.CompilerParams(
+            collective_id=0, has_side_effects=True, vmem_limit_bytes=56 * 2**20
+        ),
+        name="window_attention",
+    )(queries, keys, values, doc_lengths)
+
+
+def window_fits(n_grp, n_cp, queries, keys):
+    line = 2 * keys.shape[0] * keys.shape[1] // n_grp * keys.shape[2] * keys.dtype.itemsize
+    return n_cp % 2 == 0 and n_cp >= 4 and n_grp >= 3 and line <= WINDOW_BYTES
 
 
 def doc_of(positions, ends):
@@ -123,16 +371,25 @@
 
 
 def solution(mesh):
+    n_grp, n_cp = mesh.shape["grp"], mesh.shape["cp"]
     placed = (
         P(None, ("grp", "cp"), None),
         P(None, ("grp", "cp"), None),
         P(None, ("grp", "cp"), None),
         P(),
     )
-    return jax.shard_map(
-        on_device,
-        mesh=mesh,
-        in_specs=placed,
-        out_specs=P(None, ("grp", "cp"), None),
-        check_vma=False,
-    )
+
+    def run(queries, keys, values, doc_lengths):
+        if window_fits(n_grp, n_cp, queries, keys):
+            plan = functools.partial(by_window, n_grp, n_cp)
+        else:
+            plan = on_device
+        return jax.shard_map(
+            plan,
+            mesh=mesh,
+            in_specs=placed,
+            out_specs=P(None, ("grp", "cp"), None),
+            check_vma=False,
+        )(queries, keys, values, doc_lengths)
+
+    return run

time: 616 us -> 173 us (0.28)
  waiting for transfers between devices: 274 us -> 0 us
  Pallas kernels: 0 us -> 168 us
  blocking collectives: 96.8 us -> 0 us
  matrix products: 81.7 us -> 0 us
  local copies, waits for them, and re-layouts: 79.3 us -> 4.7 us
  loops' own time: 33 us -> 0 us
  other arithmetic: 32.6 us -> 0 us
  starting transfers between devices: 14.7 us -> 0 us
    all_to_all x3 -> x0, waiting for transfers between devices: 274 us -> none  [the longest x1 94.8 us: on_device(): lax.all_to_all(value_divided_rows, ('grp', 'cp'), split_axis=0, concat_ax...]
    pallas_call x0 -> x1, Pallas kernels: none -> 168 us  [by_window(): pl.pallas_call(functools.partial(window_kernel, n_grp, n_cp, streams), ou...]
    all_to_all x1 -> x0, blocking collectives: 96.8 us -> none  [on_device(): lax.all_to_all(head_output, ('grp', 'cp'), split_axis=1, concat_axis=0, t...]
    dot_general x34 -> x0, matrix products: 81.7 us -> none  [the longest x17 48.9 us: absorb(): jnp.einsum('hqk,khd->hqd', probs.astype(jnp.bfloat16), value_portion, pre...]
    another operation x9 -> x0, loops' own time: 33 us -> none  [the longest x1 31.8 us: attend_stream(): tiles = lax.map(query_span, jnp.arange(spans, dtype=jnp.int32))]
    dynamic_slice x74 -> x0, local copies, waits for them, and re-layouts: 22.5 us -> none  [the longest x8 8.61 us: query_span(): query_tile = lax.dynamic_slice_in_dim(query_seq, begin, span, 0)]
    reshape x5 -> x0, local copies, waits for them, and re-layouts: 20.5 us -> none  [the longest x2 13.5 us: by_heads(): shaped = array.reshape(n_streams, rows_per, n_ranks, per_rank, HEAD_WIDTH)]
    reduce_sum x18 -> x0, other arithmetic: 18.2 us -> none  [the longest x17 18 us: absorb(): new_sum = running_sum * factor + jnp.sum(probs, axis=-1)]
  transfers between devices with their start and end apart: 3 -> 0, of which waited for: 3 -> 0; matrix products, arithmetic and copies ran while one was open for 2% -> 0% of each run, Pallas kernels for 0% -> 0%
where the time goes in v1:
time: 173 us
  Pallas kernels  168 us (97%)
  local copies, waits for them, and re-layouts  4.7 us (3%)
    pallas_call x1, Pallas kernels, by_window(): pl.pallas_call(functools.partial(window_kernel, n_grp, n_cp, streams), ou...  168 us
    unnamed x1, local copies, waits for them, and re-layouts  4.7 us

profile of v1, /device:TPU:0, one launch (start us, length us, event | category | flops | bytes accessed | tf_op | source)
XLA Modules:
  0.0 172.9 jit_solution(9908943620543012770)
XLA Ops:
  0.0 168.2 %window_attention.1 = bf16[4,128,4096]{2,1,0:T(8,128)(2,1)} custom-call(bf16[4,128,4096]{2,1,0:T(8,128)(2,1)} %q_ref.1, bf16[4,128,1024]{2,1,0:T(8,128)(2,1)} %k_ref.1, bf16[4,128,1024]{2,1,0:T(8,128)(2,1)} %v_ref.1, s32[4,16]{1,0:T(4,128)} %len_ref.1), custom_call_target="tpu_custom_call" | custom-call | flops 9663676416 | bytes 10485760 | tf_op jit(solution)/shard_map/window_attention/pallas_call | solution.py:230
  168.2 4.7 %copy.6 = bf16[4,128,4096]{2,1,0:T(8,128)(2,1)} copy(bf16[4,128,4096]{2,1,0:T(8,128)(2,1)} %window_attention.1) | data formatting | bytes 8388608

commit v2 on v1

--- a/solution.py
+++ b/solution.py
@@ -8,7 +8,7 @@
 from jax.sharding import PartitionSpec as P
 
 MESH = pl.DeviceIdType.MESH
-PARTS = 2
+PARTS = 4
 WINDOW_BYTES = 40 * 2**20
 
 QUERY_HEADS = 32
@@ -19,7 +19,21 @@
 
 
 def window_kernel(
-    n_grp, n_cp, streams, q_ref, k_ref, v_ref, len_ref, o_ref, kv, bias, local_sem, send_sem, recv_sem
+    n_grp,
+    n_cp,
+    streams,
+    q_ref,
+    k_ref,
+    v_ref,
+    len_ref,
+    o_ref,
+    kv,
+    q_buf,
+    o_buf,
+    bias,
+    local_sem,
+    send_sem,
+    recv_sem,
 ):
     grp, cp = lax.axis_index("grp"), lax.axis_index("cp")
     z, core = cp // 2, cp % 2
@@ -29,6 +43,7 @@
     part = k_ref.shape[2] // PARTS
     heads = part // HEAD_WIDTH
     group = QUERY_HEADS // KEY_VALUE_HEADS
+    wide = part * group
     partner = (grp, z * 2 + 1 - core)
     up = (grp, cp + 2)
     down = (grp, cp - 2)
@@ -44,6 +59,17 @@
             kv.at[0, ch, :, pl.ds(which * part, part)],
             local_sem.at[which, ch],
         )
+
+    def own_columns(ch):
+        return ch // PARTS, slice(None), pl.ds(pl.multiple_of((ch % PARTS) * wide, wide), wide)
+
+    def query_copy(ch):
+        at = own_columns(ch)
+        return pltpu.make_async_copy(q_ref.at[at], q_buf.at[at], local_sem.at[2, ch])
+
+    def result_copy(ch):
+        at = own_columns(ch)
+        return pltpu.make_async_copy(o_buf.at[at], o_ref.at[at], local_sem.at[3, ch])
 
     def remote(source, target, ch, row, device):
         return pltpu.make_async_remote_copy(
@@ -62,6 +88,10 @@
     def _(ch):
         local(ch, 0).start()
         local(ch, 1).start()
+
+    @pl.loop(0, chunks)
+    def _(ch):
+        query_copy(ch).start()
 
     barrier = pltpu.get_barrier_semaphore()
 
@@ -112,29 +142,33 @@
                 allowed = allowed & (lane <= row)
             bias[:, r * rows : (r + 1) * rows] = jnp.where(allowed, 0.0, NEGATIVE)
 
-        @pl.loop(0, heads)
-        def _(head):
-            k_cols = pl.ds(pl.multiple_of(head * HEAD_WIDTH, HEAD_WIDTH), HEAD_WIDTH)
-            v_cols = pl.ds(pl.multiple_of(part + head * HEAD_WIDTH, HEAD_WIDTH), HEAD_WIDTH)
+        mask = jnp.concatenate([bias[...]] * group, axis=0)
+        query_copy(ch).wait()
+        for head in range(heads):
+            k_cols = slice(head * HEAD_WIDTH, (head + 1) * HEAD_WIDTH)
+            v_cols = slice(part + head * HEAD_WIDTH, part + (head + 1) * HEAD_WIDTH)
             k_all = jnp.concatenate([kv[r, ch, :, k_cols] for r in range(n_cp + 1)], axis=0)
             v_all = jnp.concatenate([kv[r, ch, :, v_cols] for r in range(n_cp + 1)], axis=0)
+
+            def q_cols(j):
+                at = ((piece * heads + head) * group + j) * HEAD_WIDTH
+                return pl.ds(pl.multiple_of(at, HEAD_WIDTH), HEAD_WIDTH)
+
+            scores = lax.dot_general(
+                jnp.concatenate([q_buf[stream, :, q_cols(j)] for j in range(group)], axis=0),
+                k_all,
+                (((1,), (1,)), ((), ())),
+                preferred_element_type=jnp.float32,
+            )
+            scores = scores + mask
+            largest = jnp.max(scores, axis=1, keepdims=True)
+            probs = jnp.exp2((scores - largest) * (HEAD_WIDTH**-0.5 * LOG2_E))
+            total = jnp.sum(probs, axis=1, keepdims=True)
+            summed = jnp.dot(probs.astype(jnp.bfloat16), v_all, preferred_element_type=jnp.float32)
+            result = (summed / total).astype(o_buf.dtype)
             for j in range(group):
-                at = ((piece * heads + head) * group + j) * HEAD_WIDTH
-                q_cols = pl.ds(pl.multiple_of(at, HEAD_WIDTH), HEAD_WIDTH)
-                scores = lax.dot_general(
-                    q_ref[stream, :, q_cols],
-                    k_all,
-                    (((1,), (1,)), ((), ())),
-                    preferred_element_type=jnp.float32,
-                )
-                scores = scores + bias[...]
-                largest = jnp.max(scores, axis=1, keepdims=True)
-                probs = jnp.exp2((scores - largest) * (HEAD_WIDTH**-0.5 * LOG2_E))
-                total = jnp.sum(probs, axis=1, keepdims=True)
-                summed = jnp.dot(
-                    probs.astype(jnp.bfloat16), v_all, preferred_element_type=jnp.float32
-                )
-                o_ref[stream, :, q_cols] = (summed / total).astype(o_ref.dtype)
+                o_buf[stream, :, q_cols(j)] = result[j * rows : (j + 1) * rows]
+        result_copy(ch).start()
 
     @pl.loop(0, chunks + nz)
     def _(t):
@@ -190,6 +224,7 @@
         def sent(row):
             remote(0, 1, ch, row, partner).wait_send()
 
+        result_copy(ch).wait()
         sent(hop_row)
         for d in range(nz - 1):
 
@@ -231,16 +266,18 @@
         functools.partial(window_kernel, n_grp, n_cp, streams),
         out_shape=jax.ShapeDtypeStruct(queries.shape, queries.dtype),
         in_specs=[
-            pl.BlockSpec(memory_space=pltpu.VMEM),
+            pl.BlockSpec(memory_space=pl.ANY),
             pl.BlockSpec(memory_space=pl.ANY),
             pl.BlockSpec(memory_space=pl.ANY),
             pl.BlockSpec(memory_space=pltpu.SMEM),
         ],
-        out_specs=pl.BlockSpec(memory_space=pltpu.VMEM),
+        out_specs=pl.BlockSpec(memory_space=pl.ANY),
         scratch_shapes=[
             pltpu.VMEM((n_cp + 1, chunks, rows, width), keys.dtype),
+            pltpu.VMEM(queries.shape, queries.dtype),
+            pltpu.VMEM(queries.shape, queries.dtype),
             pltpu.VMEM((rows, window), jnp.float32),
-            pltpu.SemaphoreType.DMA((2, chunks)),
+            pltpu.SemaphoreType.DMA((4, chunks)),
             pltpu.SemaphoreType.DMA((3 * nz, chunks)),
             pltpu.SemaphoreType.DMA((n_cp + 1, chunks)),
         ],

time: 173 us -> 163 us (0.942)
  Pallas kernels: 168 us -> 158 us
    pallas_call x1, Pallas kernels: 168 us -> 158 us  [by_window(): pl.pallas_call(functools.partial(window_kernel, n_grp, n_cp, streams), ou...]
where the time goes in v2:
time: 163 us
  Pallas kernels  158 us (97%)
  local copies, waits for them, and re-layouts  4.7 us (3%)
    pallas_call x1, Pallas kernels, by_window(): pl.pallas_call(functools.partial(window_kernel, n_grp, n_cp, streams), ou...  158 us
    unnamed x1, local copies, waits for them, and re-layouts  4.7 us

profile of v2, /device:TPU:0, one launch (start us, length us, event | category | flops | bytes accessed | tf_op | source)
XLA Modules:
  0.0 163.1 jit_solution(6741706409332776426)
XLA Ops:
  0.0 158.3 %window_attention.1 = bf16[4,128,4096]{2,1,0:T(8,128)(2,1)} custom-call(bf16[4,128,4096]{2,1,0:T(8,128)(2,1)} %q_ref.1, bf16[4,128,1024]{2,1,0:T(8,128)(2,1)} %k_ref.1, bf16[4,128,1024]{2,1,0:T(8,128)(2,1)} %v_ref.1, s32[4,16]{1,0:T(4,128)} %len_ref.1), custom_call_target="tpu_custom_call" | custom-call | flops 9663676416 | bytes 10485760 | tf_op jit(solution)/shard_map/window_attention/pallas_call | solution.py:265
  158.4 4.7 %copy.6 = bf16[4,128,4096]{2,1,0:T(8,128)(2,1)} copy(bf16[4,128,4096]{2,1,0:T(8,128)(2,1)} %window_attention.1) | data formatting | bytes 8388608

commit v3 on v2

--- a/solution.py
+++ b/solution.py
@@ -9,6 +9,8 @@
 
 MESH = pl.DeviceIdType.MESH
 PARTS = 4
+MOVED = 4
+OFF = 2
 WINDOW_BYTES = 40 * 2**20
 
 QUERY_HEADS = 32
@@ -38,6 +40,7 @@
     grp, cp = lax.axis_index("grp"), lax.axis_index("cp")
     z, core = cp // 2, cp % 2
     nz = n_cp // 2
+    last = nz - 1
     chunks = streams * PARTS
     rows = k_ref.shape[1]
     part = k_ref.shape[2] // PARTS
@@ -50,13 +53,23 @@
     next_line = ((grp + 1) % n_grp, cp)
     prev_line = ((grp + n_grp - 1) % n_grp, cp)
     fwd_row, hop_row, bwd_row, mate_row = 0, nz - 1, nz - 2, 2 * nz - 1
+    far_row, ahead_row, edge_row, ask_row, answer_row = (3 * nz + i for i in range(5))
+    ask_slot, answer_slot = n_cp + 2 * OFF + 1, n_cp + 2 * OFF + 2
+    at_end = (z == 0) | (z == last)
+    helper = (z == 1) | (z == last - 1)
+
+    def moved(ch):
+        return ch % MOVED == 0
+
+    def normal(ch):
+        return jnp.logical_not(moved(ch) & at_end)
 
     def local(ch, which):
         source = (k_ref, v_ref)[which]
         cols = pl.ds(pl.multiple_of((ch % PARTS) * part, part), part)
         return pltpu.make_async_copy(
             source.at[ch // PARTS, :, cols],
-            kv.at[0, ch, :, pl.ds(which * part, part)],
+            kv.at[OFF, ch, :, pl.ds(which * part, part)],
             local_sem.at[which, ch],
         )
 
@@ -64,25 +77,43 @@
         return ch // PARTS, slice(None), pl.ds(pl.multiple_of((ch % PARTS) * wide, wide), wide)
 
     def query_copy(ch):
-        at = own_columns(ch)
-        return pltpu.make_async_copy(q_ref.at[at], q_buf.at[at], local_sem.at[2, ch])
+        return pltpu.make_async_copy(q_ref.at[own_columns(ch)], q_buf.at[ch], local_sem.at[2, ch])
 
     def result_copy(ch):
-        at = own_columns(ch)
-        return pltpu.make_async_copy(o_buf.at[at], o_ref.at[at], local_sem.at[3, ch])
+        return pltpu.make_async_copy(o_buf.at[ch], o_ref.at[own_columns(ch)], local_sem.at[3, ch])
 
     def remote(source, target, ch, row, device):
         return pltpu.make_async_remote_copy(
-            src_ref=kv.at[source, ch],
-            dst_ref=kv.at[target, ch],
+            src_ref=kv.at[OFF + source, ch],
+            dst_ref=kv.at[OFF + target, ch],
             send_sem=send_sem.at[row, ch],
-            recv_sem=recv_sem.at[target, ch],
+            recv_sem=recv_sem.at[OFF + target, ch],
             device_id=device,
             device_id_type=MESH,
         )
 
     def arrived(slot, ch):
         remote(slot, slot, ch, 0, partner).wait_recv()
+
+    def ask(ch, device):
+        return pltpu.make_async_remote_copy(
+            src_ref=q_buf.at[ch],
+            dst_ref=q_buf.at[chunks + ch // MOVED],
+            send_sem=send_sem.at[ask_row, ch],
+            recv_sem=recv_sem.at[ask_slot, ch],
+            device_id=device,
+            device_id_type=MESH,
+        )
+
+    def answer(ch, device):
+        return pltpu.make_async_remote_copy(
+            src_ref=o_buf.at[chunks + ch // MOVED],
+            dst_ref=o_buf.at[ch],
+            send_sem=send_sem.at[answer_row, ch],
+            recv_sem=recv_sem.at[answer_slot, ch],
+            device_id=device,
+            device_id_type=MESH,
+        )
 
     @pl.loop(0, chunks)
     def _(ch):
@@ -102,7 +133,7 @@
     greet(next_line)
     greet(prev_line)
 
-    @pl.when(z < nz - 1)
+    @pl.when(z < last)
     def _():
         greet(up)
 
@@ -110,7 +141,6 @@
     def _():
         greet(down)
 
-    at_end = (z == 0) | (z == nz - 1)
     pl.semaphore_wait(barrier, jnp.where(at_end, 4, 5))
 
     def to_partner(d, ch):
@@ -126,9 +156,9 @@
             def _():
                 remote(2 * d, 2 * d - 1, ch, mate_row + d, partner).start()
 
-    def attend(ch):
-        stream, piece = ch // PARTS, ch % PARTS
-        base = (grp * n_cp + cp) * rows
+    def attend(ch, q_at, shift):
+        stream = ch // PARTS
+        base = (grp * n_cp + cp - shift) * rows
         row = lax.broadcasted_iota(jnp.int32, (rows, rows), 0)
         lane = lax.broadcasted_iota(jnp.int32, (rows, rows), 1)
         first = jnp.zeros((rows, rows), jnp.int32)
@@ -143,19 +173,19 @@
             bias[:, r * rows : (r + 1) * rows] = jnp.where(allowed, 0.0, NEGATIVE)
 
         mask = jnp.concatenate([bias[...]] * group, axis=0)
-        query_copy(ch).wait()
+        slots = [OFF + shift + r for r in range(n_cp + 1)]
         for head in range(heads):
             k_cols = slice(head * HEAD_WIDTH, (head + 1) * HEAD_WIDTH)
             v_cols = slice(part + head * HEAD_WIDTH, part + (head + 1) * HEAD_WIDTH)
-            k_all = jnp.concatenate([kv[r, ch, :, k_cols] for r in range(n_cp + 1)], axis=0)
-            v_all = jnp.concatenate([kv[r, ch, :, v_cols] for r in range(n_cp + 1)], axis=0)
+            k_all = jnp.concatenate([kv[slot, ch, :, k_cols] for slot in slots], axis=0)
+            v_all = jnp.concatenate([kv[slot, ch, :, v_cols] for slot in slots], axis=0)
 
             def q_cols(j):
-                at = ((piece * heads + head) * group + j) * HEAD_WIDTH
-                return pl.ds(pl.multiple_of(at, HEAD_WIDTH), HEAD_WIDTH)
+                at = (head * group + j) * HEAD_WIDTH
+                return slice(at, at + HEAD_WIDTH)
 
             scores = lax.dot_general(
-                jnp.concatenate([q_buf[stream, :, q_cols(j)] for j in range(group)], axis=0),
+                jnp.concatenate([q_buf[q_at, :, q_cols(j)] for j in range(group)], axis=0),
                 k_all,
                 (((1,), (1,)), ((), ())),
                 preferred_element_type=jnp.float32,
@@ -167,8 +197,7 @@
             summed = jnp.dot(probs.astype(jnp.bfloat16), v_all, preferred_element_type=jnp.float32)
             result = (summed / total).astype(o_buf.dtype)
             for j in range(group):
-                o_buf[stream, :, q_cols(j)] = result[j * rows : (j + 1) * rows]
-        result_copy(ch).start()
+                o_buf[q_at, :, q_cols(j)] = result[j * rows : (j + 1) * rows]
 
     @pl.loop(0, chunks + nz)
     def _(t):
@@ -176,83 +205,195 @@
         def _():
             local(t, 0).wait()
             local(t, 1).wait()
-            remote(0, 2 * nz, t, hop_row, next_line).start()
-
-            @pl.when(z < nz - 1)
+
+            @pl.when(normal(t))
+            def _():
+                remote(0, 2 * nz, t, hop_row, next_line).start()
+
+            @pl.when((z < last) & (jnp.logical_not(moved(t)) | (z < last - 1)))
             def _():
                 remote(0, 2, t, fwd_row, up).start()
 
-            to_partner(0, t)
+            @pl.when(moved(t) & (z == last))
+            def _():
+                remote(0, -2, t, ahead_row, down).start()
+
+            @pl.when(normal(t))
+            def _():
+                to_partner(0, t)
+
+            @pl.when(moved(t) & (z == last - 1) & (core == 1))
+            def _():
+                remote(0, -1, t, edge_row, partner).start()
 
         for d in range(nz, 0, -1):
             ch = t - (nz + 1 - d)
 
-            @pl.when((ch >= 0) & (ch < chunks) & (z < d))
+            @pl.when((ch >= 0) & (ch < chunks) & (z < d) & normal(ch))
             def _():
                 arrived(2 * d, ch)
                 if d > 1:
 
-                    @pl.when(z > 0)
+                    @pl.when((z > 0) & (jnp.logical_not(moved(ch)) | (z > 1)))
                     def _():
                         remote(2 * d, 2 * d - 2, ch, bwd_row + d, down).start()
 
                 to_partner(d, ch)
+                if d == nz:
+
+                    @pl.when(moved(ch) & (z == 1) & (core == 0))
+                    def _():
+                        remote(2 * nz, 2 * nz + 1, ch, edge_row, partner).start()
 
         for d in range(1, nz):
             ch = t - d
 
-            @pl.when((ch >= 0) & (ch < chunks) & (z >= d))
+            @pl.when((ch >= 0) & (ch < chunks) & (z >= d) & normal(ch))
             def _():
                 arrived(2 * d, ch)
                 if d < nz - 1:
 
-                    @pl.when(z < nz - 1)
+                    @pl.when((z < last) & (jnp.logical_not(moved(ch)) | (z < last - 1)))
                     def _():
                         remote(2 * d, 2 * d + 2, ch, fwd_row + d, up).start()
 
                 to_partner(d, ch)
-
-        @pl.when(t >= nz)
-        def _():
-            ch = t - nz
+                if d == 1:
+
+                    @pl.when(moved(ch) & (z == 1))
+                    def _():
+                        remote(2, 2 * nz + 2, ch, far_row, next_line).start()
+
+        before = t - 1
+
+        @pl.when((before >= 0) & (before < chunks) & moved(before))
+        def _():
+            @pl.when(at_end)
+            def _():
+                query_copy(before).wait()
+
+            @pl.when(z == 0)
+            def _():
+                ask(before, up).start()
+
+            @pl.when(z == last)
+            def _():
+                ask(before, down).start()
+
+            @pl.when(z == last - 1)
+            def _():
+                arrived(-2, before)
+                remote(-2, 2 * nz - 2, before, far_row, next_line).start()
+
+                @pl.when(core == 0)
+                def _():
+                    remote(-2, -1, before, edge_row, partner).start()
+
+        earlier = t - 2
+
+        @pl.when((earlier >= 0) & (earlier < chunks) & moved(earlier) & (z == 1))
+        def _():
+            arrived(2 * nz + 2, earlier)
+
+            @pl.when(core == 1)
+            def _():
+                remote(2 * nz + 2, 2 * nz + 1, earlier, edge_row, partner).start()
+
+        ch = t - nz
+
+        @pl.when((ch >= 0) & normal(ch))
+        def _():
             for d in range(nz):
                 arrived(2 * d + 1, ch)
-            attend(ch)
+            query_copy(ch).wait()
+            helps = helper & moved(ch)
+
+            @pl.when(helps)
+            def _():
+                ask(ch, partner).wait_recv()
+
+                @pl.when(z == 1)
+                def _():
+                    arrived(2 * nz + 1, ch)
+
+                @pl.when(z == last - 1)
+                def _():
+                    arrived(-1, ch)
+
+            @pl.loop(jnp.where(helps, 0, 1), 2)
+            def _(own):
+                other = 1 - own
+                attend(
+                    ch,
+                    other * (chunks + ch // MOVED) + own * ch,
+                    other * jnp.where(z == 1, 2, -2),
+                )
+
+                @pl.when(other == 1)
+                def _():
+                    @pl.when(z == 1)
+                    def _():
+                        answer(ch, down).start()
+
+                    @pl.when(z == last - 1)
+                    def _():
+                        answer(ch, up).start()
+
+            result_copy(ch).start()
 
     @pl.loop(0, chunks)
     def _(ch):
         def sent(row):
             remote(0, 1, ch, row, partner).wait_send()
 
+        @pl.when(moved(ch) & at_end)
+        def _():
+            answer(ch, partner).wait_recv()
+            result_copy(ch).start()
+            ask(ch, partner).wait_send()
+
         result_copy(ch).wait()
-        sent(hop_row)
+
+        @pl.when(moved(ch) & helper)
+        def _():
+            sent(far_row)
+            sent(edge_row)
+            answer(ch, partner).wait_send()
+
+        @pl.when(moved(ch) & (z == last))
+        def _():
+            sent(ahead_row)
+
         for d in range(nz - 1):
 
-            @pl.when((z >= d) & (z < nz - 1))
+            @pl.when((z >= d) & (z < last) & (jnp.logical_not(moved(ch)) | (z < last - 1)))
             def _():
                 sent(fwd_row + d)
 
         for d in range(2, nz + 1):
 
-            @pl.when((z < d) & (z > 0))
+            @pl.when((z < d) & (z > 0) & (jnp.logical_not(moved(ch)) | ((z > 1) & (z < last))))
             def _():
                 sent(bwd_row + d)
 
-        for d in range(nz + 1):
-            if d == 0:
-
-                @pl.when(core == 0)
-                def _():
-                    sent(mate_row)
-
-            elif d == nz:
-
-                @pl.when(core == 1)
-                def _():
-                    sent(mate_row + nz)
-
-            else:
-                sent(mate_row + d)
+        @pl.when(normal(ch))
+        def _():
+            sent(hop_row)
+            for d in range(nz + 1):
+                if d == 0:
+
+                    @pl.when(core == 0)
+                    def _():
+                        sent(mate_row)
+
+                elif d == nz:
+
+                    @pl.when(core == 1)
+                    def _():
+                        sent(mate_row + nz)
+
+                else:
+                    sent(mate_row + d)
 
 
 def by_window(n_grp, n_cp, queries, keys, values, doc_lengths):
@@ -262,6 +403,7 @@
     window = (n_cp + 1) * rows
     nz = n_cp // 2
     pairs = streams * QUERY_HEADS * rows * window
+    held = (chunks + chunks // MOVED, rows, queries.shape[2] // PARTS)
     return pl.pallas_call(
         functools.partial(window_kernel, n_grp, n_cp, streams),
         out_shape=jax.ShapeDtypeStruct(queries.shape, queries.dtype),
@@ -273,13 +415,13 @@
         ],
         out_specs=pl.BlockSpec(memory_space=pl.ANY),
         scratch_shapes=[
-            pltpu.VMEM((n_cp + 1, chunks, rows, width), keys.dtype),
-            pltpu.VMEM(queries.shape, queries.dtype),
-            pltpu.VMEM(queries.shape, queries.dtype),
+            pltpu.VMEM((n_cp + 1 + 2 * OFF, chunks, rows, width), keys.dtype),
+            pltpu.VMEM(held, queries.dtype),
+            pltpu.VMEM(held, queries.dtype),
             pltpu.VMEM((rows, window), jnp.float32),
             pltpu.SemaphoreType.DMA((4, chunks)),
-            pltpu.SemaphoreType.DMA((3 * nz, chunks)),
-            pltpu.SemaphoreType.DMA((n_cp + 1, chunks)),
+            pltpu.SemaphoreType.DMA((3 * nz + 5, chunks)),
+            pltpu.SemaphoreType.DMA((n_cp + 3 + 2 * OFF, chunks)),
         ],
         cost_estimate=pl.CostEstimate(
             flops=4 * pairs * HEAD_WIDTH, bytes_accessed=5 * queries.size, transcendentals=pairs
@@ -293,7 +435,7 @@
 
 def window_fits(n_grp, n_cp, queries, keys):
     line = 2 * keys.shape[0] * keys.shape[1] // n_grp * keys.shape[2] * keys.dtype.itemsize
-    return n_cp % 2 == 0 and n_cp >= 4 and n_grp >= 3 and line <= WINDOW_BYTES
+    return n_cp % 2 == 0 and n_cp >= 8 and n_grp >= 3 and line <= WINDOW_BYTES
 
 
 def doc_of(positions, ends):

time: 163 us -> 160 us (0.982)
  Pallas kernels: 158 us -> 155 us
    pallas_call x1, Pallas kernels: 158 us -> 155 us  [by_window(): pl.pallas_call(functools.partial(window_kernel, n_grp, n_cp, streams), ou...]
where the time goes in v3:
time: 160 us
  Pallas kernels  155 us (97%)
  local copies, waits for them, and re-layouts  4.7 us (3%)
    pallas_call x1, Pallas kernels, by_window(): pl.pallas_call(functools.partial(window_kernel, n_grp, n_cp, streams), ou...  155 us
    unnamed x1, local copies, waits for them, and re-layouts  4.7 us

profile of v3, /device:TPU:0, one launch (start us, length us, event | category | flops | bytes accessed | tf_op | source)
XLA Modules:
  0.0 160.0 jit_solution(17880125616058592435)
XLA Ops:
  0.0 155.3 %window_attention.1 = bf16[4,128,4096]{2,1,0:T(8,128)(2,1)} custom-call(bf16[4,128,4096]{2,1,0:T(8,128)(2,1)} %q_ref.1, bf16[4,128,1024]{2,1,0:T(8,128)(2,1)} %k_ref.1, bf16[4,128,1024]{2,1,0:T(8,128)(2,1)} %v_ref.1, s32[4,16]{1,0:T(4,128)} %len_ref.1), custom_call_target="tpu_custom_call" | custom-call | flops 9663676416 | bytes 10485760 | tf_op jit(solution)/shard_map/window_attention/pallas_call | solution.py:407
  155.3 4.7 %copy.6 = bf16[4,128,4096]{2,1,0:T(8,128)(2,1)} copy(bf16[4,128,4096]{2,1,0:T(8,128)(2,1)} %window_attention.1) | data formatting | bytes 8388608

commit v4 on v3

--- a/solution.py
+++ b/solution.py
@@ -9,7 +9,8 @@
 
 MESH = pl.DeviceIdType.MESH
 PARTS = 4
-MOVED = 4
+MOVED = 2
+BLOCK = 32
 OFF = 2
 WINDOW_BYTES = 40 * 2**20
 
@@ -33,6 +34,9 @@
     q_buf,
     o_buf,
     bias,
+    scores_buf,
+    weights_buf,
+    inverse_buf,
     local_sem,
     send_sem,
     recv_sem,
@@ -172,32 +176,46 @@
                 allowed = allowed & (lane <= row)
             bias[:, r * rows : (r + 1) * rows] = jnp.where(allowed, 0.0, NEGATIVE)
 
-        mask = jnp.concatenate([bias[...]] * group, axis=0)
         slots = [OFF + shift + r for r in range(n_cp + 1)]
+
+        def q_cols(head, j):
+            at = (head * group + j) * HEAD_WIDTH
+            return slice(at, at + HEAD_WIDTH)
+
         for head in range(heads):
             k_cols = slice(head * HEAD_WIDTH, (head + 1) * HEAD_WIDTH)
-            v_cols = slice(part + head * HEAD_WIDTH, part + (head + 1) * HEAD_WIDTH)
-            k_all = jnp.concatenate([kv[slot, ch, :, k_cols] for slot in slots], axis=0)
-            v_all = jnp.concatenate([kv[slot, ch, :, v_cols] for slot in slots], axis=0)
-
-            def q_cols(j):
-                at = (head * group + j) * HEAD_WIDTH
-                return slice(at, at + HEAD_WIDTH)
-
-            scores = lax.dot_general(
-                jnp.concatenate([q_buf[q_at, :, q_cols(j)] for j in range(group)], axis=0),
-                k_all,
+            scores_buf[head] = lax.dot_general(
+                jnp.concatenate([q_buf[q_at, :, q_cols(head, j)] for j in range(group)], axis=0),
+                jnp.concatenate([kv[slot, ch, :, k_cols] for slot in slots], axis=0),
                 (((1,), (1,)), ((), ())),
                 preferred_element_type=jnp.float32,
             )
-            scores = scores + mask
-            largest = jnp.max(scores, axis=1, keepdims=True)
-            probs = jnp.exp2((scores - largest) * (HEAD_WIDTH**-0.5 * LOG2_E))
-            total = jnp.sum(probs, axis=1, keepdims=True)
-            summed = jnp.dot(probs.astype(jnp.bfloat16), v_all, preferred_element_type=jnp.float32)
-            result = (summed / total).astype(o_buf.dtype)
+
+        def normalise(i, carry):
+            at = pl.ds(pl.multiple_of(i * BLOCK, BLOCK), BLOCK)
+            token = pl.ds(pl.multiple_of(i % (rows // BLOCK) * BLOCK, BLOCK), BLOCK)
+            mask = bias[token, :]
+            for head in range(heads):
+                scores = scores_buf[head, at, :] + mask
+                largest = jnp.max(scores, axis=1, keepdims=True)
+                probs = jnp.exp2((scores - largest) * (HEAD_WIDTH**-0.5 * LOG2_E))
+                total = jnp.sum(probs, axis=1, keepdims=True)
+                weights_buf[head, at, :] = probs.astype(jnp.bfloat16)
+                inverse_buf[head, at, :] = jnp.broadcast_to(1.0 / total, (BLOCK, HEAD_WIDTH))
+            return carry
+
+        lax.fori_loop(0, group * rows // BLOCK, normalise, 0, unroll=2)
+
+        for head in range(heads):
+            v_cols = slice(part + head * HEAD_WIDTH, part + (head + 1) * HEAD_WIDTH)
+            summed = jnp.dot(
+                weights_buf[head],
+                jnp.concatenate([kv[slot, ch, :, v_cols] for slot in slots], axis=0),
+                preferred_element_type=jnp.float32,
+            )
+            result = (summed * inverse_buf[head]).astype(o_buf.dtype)
             for j in range(group):
-                o_buf[q_at, :, q_cols(j)] = result[j * rows : (j + 1) * rows]
+                o_buf[q_at, :, q_cols(head, j)] = result[j * rows : (j + 1) * rows]
 
     @pl.loop(0, chunks + nz)
     def _(t):
@@ -403,6 +421,8 @@
     window = (n_cp + 1) * rows
     nz = n_cp // 2
     pairs = streams * QUERY_HEADS * rows * window
+    heads = KEY_VALUE_HEADS // PARTS
+    stacked = rows * QUERY_HEADS // KEY_VALUE_HEADS
     held = (chunks + chunks // MOVED, rows, queries.shape[2] // PARTS)
     return pl.pallas_call(
         functools.partial(window_kernel, n_grp, n_cp, streams),
@@ -419,6 +439,9 @@
             pltpu.VMEM(held, queries.dtype),
             pltpu.VMEM(held, queries.dtype),
             pltpu.VMEM((rows, window), jnp.float32),
+            pltpu.VMEM((heads, stacked, window), jnp.float32),
+            pltpu.VMEM((heads, stacked, window), jnp.bfloat16),
+            pltpu.VMEM((heads, stacked, HEAD_WIDTH), jnp.float32),
             pltpu.SemaphoreType.DMA((4, chunks)),
             pltpu.SemaphoreType.DMA((3 * nz + 5, chunks)),
             pltpu.SemaphoreType.DMA((n_cp + 3 + 2 * OFF, chunks)),

time: 160 us -> 152 us (0.950)
  Pallas kernels: 155 us -> 146 us
    pallas_call x1, Pallas kernels: 155 us -> 146 us  [by_window(): pl.pallas_call(functools.partial(window_kernel, n_grp, n_cp, streams), ou...]
where the time goes in v4:
time: 152 us; the launch traced here: 151 us
  Pallas kernels  146 us (96%)
  local copies, waits for them, and re-layouts  4.7 us (3%)
    pallas_call x1, Pallas kernels, by_window(): pl.pallas_call(functools.partial(window_kernel, n_grp, n_cp, streams), ou...  146 us
    unnamed x1, local copies, waits for them, and re-layouts  4.7 us

profile of v4, /device:TPU:0, one launch (start us, length us, event | category | flops | bytes accessed | tf_op | source)
XLA Modules:
  0.0 151.1 jit_solution(14692330035179098518)
XLA Ops:
  0.0 146.4 %window_attention.1 = bf16[4,128,4096]{2,1,0:T(8,128)(2,1)} custom-call(bf16[4,128,4096]{2,1,0:T(8,128)(2,1)} %q_ref.1, bf16[4,128,1024]{2,1,0:T(8,128)(2,1)} %k_ref.1, bf16[4,128,1024]{2,1,0:T(8,128)(2,1)} %v_ref.1, s32[4,16]{1,0:T(4,128)} %len_ref.1), custom_call_target="tpu_custom_call" | custom-call | flops 9663676416 | bytes 10485760 | tf_op jit(solution)/shard_map/window_attention/pallas_call | solution.py:427
  146.4 4.7 %copy.6 = bf16[4,128,4096]{2,1,0:T(8,128)(2,1)} copy(bf16[4,128,4096]{2,1,0:T(8,128)(2,1)} %window_attention.1) | data formatting | bytes 8388608

commit v5 on v4

--- a/solution.py
+++ b/solution.py
@@ -63,7 +63,7 @@
     helper = (z == 1) | (z == last - 1)
 
     def moved(ch):
-        return ch % MOVED == 0
+        return (ch % MOVED == 1) & (ch > MOVED) & (ch < chunks - 1)
 
     def normal(ch):
         return jnp.logical_not(moved(ch) & at_end)
@@ -217,35 +217,42 @@
             for j in range(group):
                 o_buf[q_at, :, q_cols(head, j)] = result[j * rows : (j + 1) * rows]
 
-    @pl.loop(0, chunks + nz)
+    def ahead(ch):
+        local(ch, 0).wait()
+        local(ch, 1).wait()
+
+        @pl.when(normal(ch))
+        def _():
+            remote(0, 2 * nz, ch, hop_row, next_line).start()
+
+        @pl.when(moved(ch) & (z == last))
+        def _():
+            remote(0, -2, ch, ahead_row, down).start()
+
+    ahead(0)
+
+    @pl.loop(0, chunks + nz - 1)
     def _(t):
         @pl.when(t < chunks)
         def _():
-            local(t, 0).wait()
-            local(t, 1).wait()
+            @pl.when((z < last) & (jnp.logical_not(moved(t)) | (z < last - 1)))
+            def _():
+                remote(0, 2, t, fwd_row, up).start()
 
             @pl.when(normal(t))
             def _():
-                remote(0, 2 * nz, t, hop_row, next_line).start()
-
-            @pl.when((z < last) & (jnp.logical_not(moved(t)) | (z < last - 1)))
-            def _():
-                remote(0, 2, t, fwd_row, up).start()
-
-            @pl.when(moved(t) & (z == last))
-            def _():
-                remote(0, -2, t, ahead_row, down).start()
-
-            @pl.when(normal(t))
-            def _():
                 to_partner(0, t)
 
             @pl.when(moved(t) & (z == last - 1) & (core == 1))
             def _():
                 remote(0, -1, t, edge_row, partner).start()
 
+        @pl.when(t + 1 < chunks)
+        def _():
+            ahead(t + 1)
+
         for d in range(nz, 0, -1):
-            ch = t - (nz + 1 - d)
+            ch = t - (nz - d)
 
             @pl.when((ch >= 0) & (ch < chunks) & (z < d) & normal(ch))
             def _():
@@ -298,14 +305,14 @@
             def _():
                 ask(before, down).start()
 
-            @pl.when(z == last - 1)
-            def _():
-                arrived(-2, before)
-                remote(-2, 2 * nz - 2, before, far_row, next_line).start()
-
-                @pl.when(core == 0)
-                def _():
-                    remote(-2, -1, before, edge_row, partner).start()
+        @pl.when((t < chunks) & moved(t) & (z == last - 1))
+        def _():
+            arrived(-2, t)
+            remote(-2, 2 * nz - 2, t, far_row, next_line).start()
+
+            @pl.when(core == 0)
+            def _():
+                remote(-2, -1, t, edge_row, partner).start()
 
         earlier = t - 2
 
@@ -317,7 +324,7 @@
             def _():
                 remote(2 * nz + 2, 2 * nz + 1, earlier, edge_row, partner).start()
 
-        ch = t - nz
+        ch = t - (nz - 1)
 
         @pl.when((ch >= 0) & normal(ch))
         def _():

time: 152 us -> 160 us (1.053)
  Pallas kernels: 146 us -> 155 us
    pallas_call x1, Pallas kernels: 146 us -> 155 us  [by_window(): pl.pallas_call(functools.partial(window_kernel, n_grp, n_cp, streams), ou...]
where the time goes in v5:
time: 160 us
  Pallas kernels  155 us (97%)
  local copies, waits for them, and re-layouts  4.7 us (3%)
    pallas_call x1, Pallas kernels, by_window(): pl.pallas_call(functools.partial(window_kernel, n_grp, n_cp, streams), ou...  155 us
    unnamed x1, local copies, waits for them, and re-layouts  4.7 us

profile of v5, /device:TPU:0, one launch (start us, length us, event | category | flops | bytes accessed | tf_op | source)
XLA Modules:
  0.0 159.6 jit_solution(5968492692293923000)
XLA Ops:
  0.0 154.9 %window_attention.1 = bf16[4,128,4096]{2,1,0:T(8,128)(2,1)} custom-call(bf16[4,128,4096]{2,1,0:T(8,128)(2,1)} %q_ref.1, bf16[4,128,1024]{2,1,0:T(8,128)(2,1)} %k_ref.1, bf16[4,128,1024]{2,1,0:T(8,128)(2,1)} %v_ref.1, s32[4,16]{1,0:T(4,128)} %len_ref.1), custom_call_target="tpu_custom_call" | custom-call | flops 9663676416 | bytes 10485760 | tf_op jit(solution)/shard_map/window_attention/pallas_call | solution.py:434
  154.9 4.7 %copy.6 = bf16[4,128,4096]{2,1,0:T(8,128)(2,1)} copy(bf16[4,128,4096]{2,1,0:T(8,128)(2,1)} %window_attention.1) | data formatting | bytes 8388608

commit v6 on v5

--- a/solution.py
+++ b/solution.py
@@ -63,7 +63,7 @@
     helper = (z == 1) | (z == last - 1)
 
     def moved(ch):
-        return (ch % MOVED == 1) & (ch > MOVED) & (ch < chunks - 1)
+        return (ch % MOVED == 0) & (ch > 0)
 
     def normal(ch):
         return jnp.logical_not(moved(ch) & at_end)
@@ -231,7 +231,7 @@
 
     ahead(0)
 
-    @pl.loop(0, chunks + nz - 1)
+    @pl.loop(0, chunks + nz)
     def _(t):
         @pl.when(t < chunks)
         def _():
@@ -289,7 +289,7 @@
                     def _():
                         remote(2, 2 * nz + 2, ch, far_row, next_line).start()
 
-        before = t - 1
+        before = t - 2
 
         @pl.when((before >= 0) & (before < chunks) & moved(before))
         def _():
@@ -324,16 +324,22 @@
             def _():
                 remote(2 * nz + 2, 2 * nz + 1, earlier, edge_row, partner).start()
 
-        ch = t - (nz - 1)
-
-        @pl.when((ch >= 0) & normal(ch))
-        def _():
-            for d in range(nz):
-                arrived(2 * d + 1, ch)
-            query_copy(ch).wait()
-            helps = helper & moved(ch)
-
-            @pl.when(helps)
+        mine, theirs = t - (nz - 1), t - nz
+        attends = (mine >= 0) & (mine < chunks) & normal(mine)
+        helps = (theirs >= 0) & helper & moved(theirs)
+
+        @pl.loop(jnp.where(helps, 0, 1), jnp.where(attends, 2, 1))
+        def _(own):
+            other = 1 - own
+            ch = theirs + own
+
+            @pl.when(own == 1)
+            def _():
+                for d in range(nz):
+                    arrived(2 * d + 1, ch)
+                query_copy(ch).wait()
+
+            @pl.when(other == 1)
             def _():
                 ask(ch, partner).wait_recv()
 
@@ -345,26 +351,23 @@
                 def _():
                     arrived(-1, ch)
 
-            @pl.loop(jnp.where(helps, 0, 1), 2)
-            def _(own):
-                other = 1 - own
-                attend(
-                    ch,
-                    other * (chunks + ch // MOVED) + own * ch,
-                    other * jnp.where(z == 1, 2, -2),
-                )
-
-                @pl.when(other == 1)
-                def _():
-                    @pl.when(z == 1)
-                    def _():
-                        answer(ch, down).start()
-
-                    @pl.when(z == last - 1)
-                    def _():
-                        answer(ch, up).start()
-
-            result_copy(ch).start()
+            attend(
+                ch,
+                other * (chunks + ch // MOVED) + own * ch,
+                other * jnp.where(z == 1, 2, -2),
+            )
+
+            @pl.when(own == 1)
+            def _():
+                result_copy(ch).start()
+
+            @pl.when((other == 1) & (z == 1))
+            def _():
+                answer(ch, down).start()
+
+            @pl.when((other == 1) & (z == last - 1))
+            def _():
+                answer(ch, up).start()
 
     @pl.loop(0, chunks)
     def _(ch):

time: 160 us -> 157 us (0.981)
  Pallas kernels: 155 us -> 152 us
    pallas_call x1, Pallas kernels: 155 us -> 152 us  [by_window(): pl.pallas_call(functools.partial(window_kernel, n_grp, n_cp, streams), ou...]
where the time goes in v6:
time: 157 us
  Pallas kernels  152 us (97%)
  local copies, waits for them, and re-layouts  4.7 us (3%)
    pallas_call x1, Pallas kernels, by_window(): pl.pallas_call(functools.partial(window_kernel, n_grp, n_cp, streams), ou...  152 us
    unnamed x1, local copies, waits for them, and re-layouts  4.7 us

profile of v6, /device:TPU:0, one launch (start us, length us, event | category | flops | bytes accessed | tf_op | source)
XLA Modules:
  0.0 156.8 jit_solution(6618323652917719924)
XLA Ops:
  0.0 152.1 %window_attention.1 = bf16[4,128,4096]{2,1,0:T(8,128)(2,1)} custom-call(bf16[4,128,4096]{2,1,0:T(8,128)(2,1)} %q_ref.1, bf16[4,128,1024]{2,1,0:T(8,128)(2,1)} %k_ref.1, bf16[4,128,1024]{2,1,0:T(8,128)(2,1)} %v_ref.1, s32[4,16]{1,0:T(4,128)} %len_ref.1), custom_call_target="tpu_custom_call" | custom-call | flops 9663676416 | bytes 10485760 | tf_op jit(solution)/shard_map/window_attention/pallas_call | solution.py:437
  152.1 4.7 %copy.6 = bf16[4,128,4096]{2,1,0:T(8,128)(2,1)} copy(bf16[4,128,4096]{2,1,0:T(8,128)(2,1)} %window_attention.1) | data formatting | bytes 8388608

commit v7 on v4

--- a/solution.py
+++ b/solution.py
@@ -217,7 +217,9 @@
             for j in range(group):
                 o_buf[q_at, :, q_cols(head, j)] = result[j * rows : (j + 1) * rows]
 
-    @pl.loop(0, chunks + nz)
+    lag = jnp.maximum(2 * (nz - z), 2 * z)
+
+    @pl.loop(0, chunks + 2 * nz)
     def _(t):
         @pl.when(t < chunks)
         def _():
@@ -245,7 +247,7 @@
                 remote(0, -1, t, edge_row, partner).start()
 
         for d in range(nz, 0, -1):
-            ch = t - (nz + 1 - d)
+            ch = t - 2 * (nz + 1 - d)
 
             @pl.when((ch >= 0) & (ch < chunks) & (z < d) & normal(ch))
             def _():
@@ -264,7 +266,7 @@
                         remote(2 * nz, 2 * nz + 1, ch, edge_row, partner).start()
 
         for d in range(1, nz):
-            ch = t - d
+            ch = t - 2 * d
 
             @pl.when((ch >= 0) & (ch < chunks) & (z >= d) & normal(ch))
             def _():
@@ -298,17 +300,19 @@
             def _():
                 ask(before, down).start()
 
-            @pl.when(z == last - 1)
-            def _():
-                arrived(-2, before)
-                remote(-2, 2 * nz - 2, before, far_row, next_line).start()
-
-                @pl.when(core == 0)
-                def _():
-                    remote(-2, -1, before, edge_row, partner).start()
-
         earlier = t - 2
 
+        @pl.when((earlier >= 0) & (earlier < chunks) & moved(earlier) & (z == last - 1))
+        def _():
+            arrived(-2, earlier)
+            remote(-2, 2 * nz - 2, earlier, far_row, next_line).start()
+
+            @pl.when(core == 0)
+            def _():
+                remote(-2, -1, earlier, edge_row, partner).start()
+
+        earlier = t - 4
+
         @pl.when((earlier >= 0) & (earlier < chunks) & moved(earlier) & (z == 1))
         def _():
             arrived(2 * nz + 2, earlier)
@@ -317,9 +321,9 @@
             def _():
                 remote(2 * nz + 2, 2 * nz + 1, earlier, edge_row, partner).start()
 
-        ch = t - nz
-
-        @pl.when((ch >= 0) & normal(ch))
+        ch = t - lag
+
+        @pl.when((ch >= 0) & (ch < chunks) & normal(ch))
         def _():
             for d in range(nz):
                 arrived(2 * d + 1, ch)

time: 152 us -> 170 us (1.12)
  Pallas kernels: 146 us -> 164 us
    pallas_call x1, Pallas kernels: 146 us -> 164 us  [by_window(): pl.pallas_call(functools.partial(window_kernel, n_grp, n_cp, streams), ou...]
where the time goes in v7:
time: 170 us; the launch traced here: 169 us
  Pallas kernels  164 us (96%)
  local copies, waits for them, and re-layouts  4.7 us (3%)
    pallas_call x1, Pallas kernels, by_window(): pl.pallas_call(functools.partial(window_kernel, n_grp, n_cp, streams), ou...  164 us
    unnamed x1, local copies, waits for them, and re-layouts  4.7 us

profile of v7, /device:TPU:0, one launch (start us, length us, event | category | flops | bytes accessed | tf_op | source)
XLA Modules:
  0.0 168.9 jit_solution(6062354595131613762)
XLA Ops:
  0.0 164.2 %window_attention.1 = bf16[4,128,4096]{2,1,0:T(8,128)(2,1)} custom-call(bf16[4,128,4096]{2,1,0:T(8,128)(2,1)} %q_ref.1, bf16[4,128,1024]{2,1,0:T(8,128)(2,1)} %k_ref.1, bf16[4,128,1024]{2,1,0:T(8,128)(2,1)} %v_ref.1, s32[4,16]{1,0:T(4,128)} %len_ref.1), custom_call_target="tpu_custom_call" | custom-call | flops 9663676416 | bytes 10485760 | tf_op jit(solution)/shard_map/window_attention/pallas_call | solution.py:431
  164.2 4.7 %copy.6 = bf16[4,128,4096]{2,1,0:T(8,128)(2,1)} copy(bf16[4,128,4096]{2,1,0:T(8,128)(2,1)} %window_attention.1) | data formatting | bytes 8388608
